TPU v7x, 256 devices: a whole 4x4x8 slice. The times are simulated.
256 devices in a mesh: batch: 16 (over x, y), layer: 16 (over z, core).
Axes of the slice: x: 4, y: 4, z: 8, core: 2. Of those that a mesh axis runs over, the one named last changes fastest.
Arguments:
- inputs: float32 [256, 4096], P(None, 'batch'), parts along dimension 1, may hold values from -6 to 6
- guess: float32 [16, 256, 4096], P('layer', None, 'batch'), parts along dimension 2, may hold values from -6 to 6
- weights: bfloat16 [64, 256, 2304], P('layer'), may hold values from -0.125 to 0.125
Outputs:
- states: float32 [64, 256, 4096], P('layer', None, 'batch'), parts along dimension 2
There are 16 independent parts, one for each index of `batch`. A program takes and returns all parts, laid end to end along the dimension named above; an argument that names none is the same for every part. Nothing has to cross between parts.
All inputs are finite; a program needn't handle non-finite values.
Results may differ from a plain program's by a relative error of at most 0.01.
Values may be sent and summed in bfloat16 or wider, within the bound.
No kernel may reach another device: no remote copies, remote signals or barrier semaphores. Data moves between devices by JAX's collectives and lax.ppermute only.
A program may use at most 64 MiB of HBM per device.

v0:
```python
import jax
import jax.numpy as jnp
from jax import lax
from jax.sharding import PartitionSpec as P

HEIGHT = 16
WIDTH = 16
COARSEN = 4


def passed_along(x, axis, by):
    size = lax.axis_size(axis)
    pairs = [(i, i + by) for i in range(size) if 0 <= i + by < size]
    return lax.ppermute(x, axis, pairs)


def convolve(weight, state):
    chans = state.shape[0]
    grid = state.astype(jnp.bfloat16).reshape(chans, HEIGHT, WIDTH)
    padded = jnp.pad(grid, ((0, 0), (1, 1), (1, 1)))
    pieces = [
        padded[:, 1 + rowoff : 1 + rowoff + HEIGHT, 1 + coloff : 1 + coloff + WIDTH]
        for rowoff in (-1, 0, 1)
        for coloff in (-1, 0, 1)
    ]
    stacked = jnp.concatenate(pieces, 0).reshape(9 * chans, HEIGHT * WIDTH)
    return jnp.dot(weight, stacked, preferred_element_type=jnp.float32)


def advance(weight, state, factor):
    return state + factor * jnp.tanh(convolve(weight, state))


def per_device(inputs, guess, weights):
    position = lax.axis_index("layer")
    devices = lax.axis_size("layer")
    first_w = weights[0]

    def fine_sweep(left):
        result = []
        state = left
        for inner in range(COARSEN - 1):
            state = advance(weights[inner], state, 0.25)
            result.append(state)
        return result

    left = jnp.where(position == 0, inputs, guess[0])
    interior = fine_sweep(left)
    cpoint = advance(weights[COARSEN - 1], interior[-1], 0.25)
    previous = passed_along(cpoint, "layer", 1)
    left = jnp.where(position == 0, inputs, previous)
    interior = fine_sweep(left)
    resid = advance(weights[COARSEN - 1], interior[-1], 0.25) - cpoint
    restricted = cpoint
    rhs = restricted - advance(first_w, left, 1.0) + resid

    def coarse_left(values):
        arrived = passed_along(values, "layer", 1)
        return jnp.where(position == 0, inputs, arrived)

    def relax(values, phases):
        for phase in phases:
            update = advance(first_w, coarse_left(values), 1.0) + rhs
            values = jnp.where(position % COARSEN == phase, update, values)
        return values

    phases = list(range(COARSEN - 1))
    coarse = relax(restricted, phases + [COARSEN - 1] + phases)
    second = rhs - (coarse - advance(first_w, coarse_left(coarse), 1.0))
    upper = coarse
    owner = position % COARSEN == COARSEN - 1
    relay = jnp.where(position == 0, inputs, upper)
    upper_prev = upper
    for step in range(COARSEN):
        arrived = passed_along(relay, "layer", 1)
        upper_prev = jnp.where(position == 0, inputs, arrived)
        relay = jnp.where(owner, upper, upper_prev)
    coarse_rhs = upper - advance(first_w, upper_prev, 4.0) + second

    def owner_step(value):
        return advance(first_w, value, 4.0) + coarse_rhs

    def keep_value(value):
        return value

    def one_turn(turn, carry):
        arrived = passed_along(carry, "layer", 1)
        active = position == turn
        update = lax.cond(jnp.logical_and(active, owner), owner_step, keep_value, arrived)
        return jnp.where(active, update, carry)

    solved = lax.fori_loop(1, devices, one_turn, inputs)
    coarse = jnp.where(owner, coarse + solved - upper, coarse)
    coarse = relax(coarse, phases)
    cpoint = cpoint + coarse - restricted
    previous = passed_along(cpoint, "layer", 1)
    left = jnp.where(position == 0, inputs, previous)
    interior = fine_sweep(left)
    return jnp.stack(interior + [cpoint], 0)


def solution(mesh):
    return jax.shard_map(
        per_device,
        mesh=mesh,
        in_specs=(P(None, "batch"), P("layer", None, "batch"), P("layer", None, None)),
        out_specs=P("layer", None, "batch"),
        check_vma=False,
    )
```

profile of v0, /device:TPU:138, one launch (start us, length us, event | category | flops | bytes accessed | tf_op | source)
XLA Modules:
  0.0 299.2 jit_solution(10120103523434824276)
XLA Ops:
  9.3 7.0 %collective-permute-done.1 = f32[256,256]{0,1:T(8,128)S(1)} collective-permute-done((f32[256,256]{0,1:T(8,128)S(1)}, f32[256,256]{0,1:T(8,128)S(1)}, u32[]{:S(2)}, u32[]{:S(2)}) %collective-permute-start.1) | collective-permute-done | bytes 262176 | tf_op jit(solution)/shard_map/ppermute | solution.py:14
  23.1 7.0 %collective-permute-done.2 = f32[256,256]{0,1:T(8,128)S(1)} collective-permute-done((f32[256,256]{0,1:T(8,128)S(1)}, f32[256,256]{0,1:T(8,128)S(1)}, u32[]{:S(2)}, u32[]{:S(2)}) %collective-permute-start.2) | collective-permute-done | bytes 262176 | tf_op jit(solution)/shard_map/ppermute | solution.py:14
  34.1 7.0 %collective-permute-done.3 = f32[256,256]{0,1:T(8,128)S(1)} collective-permute-done((f32[256,256]{0,1:T(8,128)S(1)}, f32[256,256]{0,1:T(8,128)S(1)}, u32[]{:S(2)}, u32[]{:S(2)}) %collective-permute-start.3) | collective-permute-done | bytes 262176 | tf_op jit(solution)/shard_map/ppermute | solution.py:14
  45.2 7.0 %collective-permute-done.4 = f32[256,256]{0,1:T(8,128)S(1)} collective-permute-done((f32[256,256]{0,1:T(8,128)S(1)}, f32[256,256]{0,1:T(8,128)S(1)}, u32[]{:S(2)}, u32[]{:S(2)}) %collective-permute-start.4) | collective-permute-done | bytes 262176 | tf_op jit(solution)/shard_map/ppermute | solution.py:14
  56.3 7.0 %collective-permute-done.5 = f32[256,256]{0,1:T(8,128)S(1)} collective-permute-done((f32[256,256]{0,1:T(8,128)S(1)}, f32[256,256]{0,1:T(8,128)S(1)}, u32[]{:S(2)}, u32[]{:S(2)}) %collective-permute-start.5) | collective-permute-done | bytes 262176 | tf_op jit(solution)/shard_map/ppermute | solution.py:14
  66.1 7.0 %collective-permute-done.6 = f32[256,256]{0,1:T(8,128)S(1)} collective-permute-done((f32[256,256]{0,1:T(8,128)S(1)}, f32[256,256]{0,1:T(8,128)S(1)}, u32[]{:S(2)}, u32[]{:S(2)}) %collective-permute-start.6) | collective-permute-done | bytes 262176 | tf_op jit(solution)/shard_map/ppermute | solution.py:14
  75.9 7.0 %collective-permute-done.7 = f32[256,256]{0,1:T(8,128)S(1)} collective-permute-done((f32[256,256]{0,1:T(8,128)S(1)}, f32[256,256]{0,1:T(8,128)S(1)}, u32[]{:S(2)}, u32[]{:S(2)}) %collective-permute-start.7) | collective-permute-done | bytes 262176 | tf_op jit(solution)/shard_map/ppermute | solution.py:14
  85.6 7.0 %collective-permute-done.8 = f32[256,256]{0,1:T(8,128)S(1)} collective-permute-done((f32[256,256]{0,1:T(8,128)S(1)}, f32[256,256]{0,1:T(8,128)S(1)}, u32[]{:S(2)}, u32[]{:S(2)}) %collective-permute-start.8) | collective-permute-done | bytes 262176 | tf_op jit(solution)/shard_map/ppermute | solution.py:14
  94.6 7.0 %collective-permute-done.9 = f32[256,256]{0,1:T(8,128)S(1)} collective-permute-done((f32[256,256]{0,1:T(8,128)S(1)}, f32[256,256]{0,1:T(8,128)S(1)}, u32[]{:S(2)}, u32[]{:S(2)}) %collective-permute-start.9) | collective-permute-done | bytes 262176 | tf_op jit(solution)/shard_map/ppermute | solution.py:14
  105.5 5.0 %collective-permute-done.10 = f32[256,256]{0,1:T(8,128)S(1)} collective-permute-done((f32[256,256]{0,1:T(8,128)S(1)}, f32[256,256]{0,1:T(8,128)S(1)}, u32[]{:S(2)}, u32[]{:S(2)}) %collective-permute-start.10) | collective-permute-done | bytes 262176 | tf_op jit(solution)/shard_map/ppermute | solution.py:14
  110.6 2.1 collective-permute-start.11
  113.3 6.1 %collective-permute-done.11 = f32[256,256]{0,1:T(8,128)S(1)} collective-permute-done((f32[256,256]{0,1:T(8,128)S(1)}, f32[256,256]{0,1:T(8,128)S(1)}, u32[]{:S(2)}, u32[]{:S(2)}) %collective-permute-start.11) | collective-permute-done | bytes 262176 | tf_op jit(solution)/shard_map/ppermute | solution.py:14
  121.2 134.5 %while.13 = (s32[]{:T(128)}, f32[256,256]{0,1:T(8,128)S(1)}, s32[]{:T(128)}, pred[]{:T(512)}, bf16[256,2304]{1,0:T(8,128)(2,1)S(1)}, /*index=5*/f32[256,256]{0,1:T(8,128)S(1)}, s32[]{:T(128)}) while((s32[]{:T(128)}, f32[256,256]{0,1:T(8,128)S(1)}, s32[]{:T(128)}, pred[]{:T(512)}, bf16[256,2304]{1,0:T(8,128)(2,1)S(1)}, ...), condition=%wide.region_3.4_spmd, body=%wide.region_0.3_spmd.sunk | while | flops 302383104 | bytes 9044135 | solution.py:92
  123.1 7.0 %collective-permute-done = f32[256,256]{0,1:T(8,128)S(1)} collective-permute-done((f32[256,256]{0,1:T(8,128)S(1)}, f32[256,256]{0,1:T(8,128)S(1)}, u32[]{:S(2)}, u32[]{:S(2)}) %collective-permute-start) | collective-permute-done | bytes 262176 | tf_op jit(solution)/shard_map/while/body/eval_jaxpr/ppermute | solution.py:14
  132.1 7.0 %collective-permute-done = f32[256,256]{0,1:T(8,128)S(1)} collective-permute-done((f32[256,256]{0,1:T(8,128)S(1)}, f32[256,256]{0,1:T(8,128)S(1)}, u32[]{:S(2)}, u32[]{:S(2)}) %collective-permute-start) | collective-permute-done | bytes 262176 | tf_op jit(solution)/shard_map/while/body/eval_jaxpr/ppermute | solution.py:14
  141.0 7.0 %collective-permute-done = f32[256,256]{0,1:T(8,128)S(1)} collective-permute-done((f32[256,256]{0,1:T(8,128)S(1)}, f32[256,256]{0,1:T(8,128)S(1)}, u32[]{:S(2)}, u32[]{:S(2)}) %collective-permute-start) | collective-permute-done | bytes 262176 | tf_op jit(solution)/shard_map/while/body/eval_jaxpr/ppermute | solution.py:14
  150.0 7.0 %collective-permute-done = f32[256,256]{0,1:T(8,128)S(1)} collective-permute-done((f32[256,256]{0,1:T(8,128)S(1)}, f32[256,256]{0,1:T(8,128)S(1)}, u32[]{:S(2)}, u32[]{:S(2)}) %collective-permute-start) | collective-permute-done | bytes 262176 | tf_op jit(solution)/shard_map/while/body/eval_jaxpr/ppermute | solution.py:14
  159.0 7.0 %collective-permute-done = f32[256,256]{0,1:T(8,128)S(1)} collective-permute-done((f32[256,256]{0,1:T(8,128)S(1)}, f32[256,256]{0,1:T(8,128)S(1)}, u32[]{:S(2)}, u32[]{:S(2)}) %collective-permute-start) | collective-permute-done | bytes 262176 | tf_op jit(solution)/shard_map/while/body/eval_jaxpr/ppermute | solution.py:14
  167.9 7.0 %collective-permute-done = f32[256,256]{0,1:T(8,128)S(1)} collective-permute-done((f32[256,256]{0,1:T(8,128)S(1)}, f32[256,256]{0,1:T(8,128)S(1)}, u32[]{:S(2)}, u32[]{:S(2)}) %collective-permute-start) | collective-permute-done | bytes 262176 | tf_op jit(solution)/shard_map/while/body/eval_jaxpr/ppermute | solution.py:14
  176.9 7.0 %collective-permute-done = f32[256,256]{0,1:T(8,128)S(1)} collective-permute-done((f32[256,256]{0,1:T(8,128)S(1)}, f32[256,256]{0,1:T(8,128)S(1)}, u32[]{:S(2)}, u32[]{:S(2)}) %collective-permute-start) | collective-permute-done | bytes 262176 | tf_op jit(solution)/shard_map/while/body/eval_jaxpr/ppermute | solution.py:14
  185.9 7.0 %collective-permute-done = f32[256,256]{0,1:T(8,128)S(1)} collective-permute-done((f32[256,256]{0,1:T(8,128)S(1)}, f32[256,256]{0,1:T(8,128)S(1)}, u32[]{:S(2)}, u32[]{:S(2)}) %collective-permute-start) | collective-permute-done | bytes 262176 | tf_op jit(solution)/shard_map/while/body/eval_jaxpr/ppermute | solution.py:14
  194.9 7.0 %collective-permute-done = f32[256,256]{0,1:T(8,128)S(1)} collective-permute-done((f32[256,256]{0,1:T(8,128)S(1)}, f32[256,256]{0,1:T(8,128)S(1)}, u32[]{:S(2)}, u32[]{:S(2)}) %collective-permute-start) | collective-permute-done | bytes 262176 | tf_op jit(solution)/shard_map/while/body/eval_jaxpr/ppermute | solution.py:14
  203.8 7.0 %collective-permute-done = f32[256,256]{0,1:T(8,128)S(1)} collective-permute-done((f32[256,256]{0,1:T(8,128)S(1)}, f32[256,256]{0,1:T(8,128)S(1)}, u32[]{:S(2)}, u32[]{:S(2)}) %collective-permute-start) | collective-permute-done | bytes 262176 | tf_op jit(solution)/shard_map/while/body/eval_jaxpr/ppermute | solution.py:14
  212.8 7.0 %collective-permute-done = f32[256,256]{0,1:T(8,128)S(1)} collective-permute-done((f32[256,256]{0,1:T(8,128)S(1)}, f32[256,256]{0,1:T(8,128)S(1)}, u32[]{:S(2)}, u32[]{:S(2)}) %collective-permute-start) | collective-permute-done | bytes 262176 | tf_op jit(solution)/shard_map/while/body/eval_jaxpr/ppermute | solution.py:14
  221.8 7.0 %collective-permute-done = f32[256,256]{0,1:T(8,128)S(1)} collective-permute-done((f32[256,256]{0,1:T(8,128)S(1)}, f32[256,256]{0,1:T(8,128)S(1)}, u32[]{:S(2)}, u32[]{:S(2)}) %collective-permute-start) | collective-permute-done | bytes 262176 | tf_op jit(solution)/shard_map/while/body/eval_jaxpr/ppermute | solution.py:14
  230.7 7.0 %collective-permute-done = f32[256,256]{0,1:T(8,128)S(1)} collective-permute-done((f32[256,256]{0,1:T(8,128)S(1)}, f32[256,256]{0,1:T(8,128)S(1)}, u32[]{:S(2)}, u32[]{:S(2)}) %collective-permute-start) | collective-permute-done | bytes 262176 | tf_op jit(solution)/shard_map/while/body/eval_jaxpr/ppermute | solution.py:14
  239.7 7.0 %collective-permute-done = f32[256,256]{0,1:T(8,128)S(1)} collective-permute-done((f32[256,256]{0,1:T(8,128)S(1)}, f32[256,256]{0,1:T(8,128)S(1)}, u32[]{:S(2)}, u32[]{:S(2)}) %collective-permute-start) | collective-permute-done | bytes 262176 | tf_op jit(solution)/shard_map/while/body/eval_jaxpr/ppermute | solution.py:14
  248.7 7.0 %collective-permute-done = f32[256,256]{0,1:T(8,128)S(1)} collective-permute-done((f32[256,256]{0,1:T(8,128)S(1)}, f32[256,256]{0,1:T(8,128)S(1)}, u32[]{:S(2)}, u32[]{:S(2)}) %collective-permute-start) | collective-permute-done | bytes 262176 | tf_op jit(solution)/shard_map/while/body/eval_jaxpr/ppermute | solution.py:14
  257.7 7.0 %collective-permute-done.13 = f32[256,256]{0,1:T(8,128)S(1)} collective-permute-done((f32[256,256]{0,1:T(8,128)S(1)}, f32[256,256]{0,1:T(8,128)S(1)}, u32[]{:S(2)}, u32[]{:S(2)}) %collective-permute-start.13) | collective-permute-done | bytes 262176 | tf_op jit(solution)/shard_map/ppermute | solution.py:14
  268.9 7.0 %collective-permute-done.14 = f32[256,256]{0,1:T(8,128)S(1)} collective-permute-done((f32[256,256]{0,1:T(8,128)S(1)}, f32[256,256]{0,1:T(8,128)S(1)}, u32[]{:S(2)}, u32[]{:S(2)}) %collective-permute-start.14) | collective-permute-done | bytes 262176 | tf_op jit(solution)/shard_map/ppermute | solution.py:14
  278.6 7.0 %collective-permute-done.15 = f32[256,256]{0,1:T(8,128)S(1)} collective-permute-done((f32[256,256]{0,1:T(8,128)S(1)}, f32[256,256]{0,1:T(8,128)S(1)}, u32[]{:S(2)}, u32[]{:S(2)}) %collective-permute-start.15) | collective-permute-done | bytes 262176 | tf_op jit(solution)/shard_map/ppermute | solution.py:14
  288.4 7.0 %collective-permute-done.16 = f32[256,256]{0,1:T(8,128)S(1)} collective-permute-done((f32[256,256]{0,1:T(8,128)S(1)}, f32[256,256]{0,1:T(8,128)S(1)}, u32[]{:S(2)}, u32[]{:S(2)}) %collective-permute-start.16) | collective-permute-done | bytes 262176 | tf_op jit(solution)/shard_map/ppermute | solution.py:14
  (342 shorter events, 88.1 us)
Async XLA Ops:
  6.8 12.0 %slice-start = ((s8[4718592]{0:T(1024)(128)(4,1)}), s8[524288]{0:T(1024)(128)(4,1)S(1)}, s32[]{:S(2)}) async-start(s8[4718592]{0:T(1024)(128)(4,1)} %bitcast.513), calls=%async_computation | async-start | bytes 1048576
  7.3 8.9 %collective-permute-start.1 = (f32[256,256]{0,1:T(8,128)S(1)}, f32[256,256]{0,1:T(8,128)S(1)}, u32[]{:S(2)}, u32[]{:S(2)}) collective-permute-start(f32[256,256]{0,1:T(8,128)S(1)} %fusion.104), channel_id=1, source_target_pairs={{0,1},{1,2},{2,3},{3,4},{4,5},{5,6},{6,7},{7,8},{8,9},{9,10},{10,1... | collective-permute-start | bytes 786440 | tf_op jit(solution)/shard_map/ppermute | solution.py:14
  21.2 8.9 %collective-permute-start.2 = (f32[256,256]{0,1:T(8,128)S(1)}, f32[256,256]{0,1:T(8,128)S(1)}, u32[]{:S(2)}, u32[]{:S(2)}) collective-permute-start(f32[256,256]{0,1:T(8,128)S(1)} %get-tuple-element.351), channel_id=1, source_target_pairs={{0,1},{1,2},{2,3},{3,4},{4,5},{5,6},{6,7},{7,8},{8,9},{9,10},{10,1... | collective-permute-start | bytes 786440 | tf_op jit(solution)/shard_map/ppermute | solution.py:14
  32.2 8.9 %collective-permute-start.3 = (f32[256,256]{0,1:T(8,128)S(1)}, f32[256,256]{0,1:T(8,128)S(1)}, u32[]{:S(2)}, u32[]{:S(2)}) collective-permute-start(f32[256,256]{0,1:T(8,128)S(1)} %fusion.159), channel_id=1, source_target_pairs={{0,1},{1,2},{2,3},{3,4},{4,5},{5,6},{6,7},{7,8},{8,9},{9,10},{10,1... | collective-permute-start | bytes 786440 | tf_op jit(solution)/shard_map/ppermute | solution.py:14
  43.2 8.9 %collective-permute-start.4 = (f32[256,256]{0,1:T(8,128)S(1)}, f32[256,256]{0,1:T(8,128)S(1)}, u32[]{:S(2)}, u32[]{:S(2)}) collective-permute-start(f32[256,256]{0,1:T(8,128)S(1)} %fusion.160), channel_id=1, source_target_pairs={{0,1},{1,2},{2,3},{3,4},{4,5},{5,6},{6,7},{7,8},{8,9},{9,10},{10,1... | collective-permute-start | bytes 786440 | tf_op jit(solution)/shard_map/ppermute | solution.py:14
  54.4 8.9 %collective-permute-start.5 = (f32[256,256]{0,1:T(8,128)S(1)}, f32[256,256]{0,1:T(8,128)S(1)}, u32[]{:S(2)}, u32[]{:S(2)}) collective-permute-start(f32[256,256]{0,1:T(8,128)S(1)} %fusion.161), channel_id=1, source_target_pairs={{0,1},{1,2},{2,3},{3,4},{4,5},{5,6},{6,7},{7,8},{8,9},{9,10},{10,1... | collective-permute-start | bytes 786440 | tf_op jit(solution)/shard_map/ppermute | solution.py:14
  64.2 8.9 %collective-permute-start.6 = (f32[256,256]{0,1:T(8,128)S(1)}, f32[256,256]{0,1:T(8,128)S(1)}, u32[]{:S(2)}, u32[]{:S(2)}) collective-permute-start(f32[256,256]{0,1:T(8,128)S(1)} %fusion.162), channel_id=1, source_target_pairs={{0,1},{1,2},{2,3},{3,4},{4,5},{5,6},{6,7},{7,8},{8,9},{9,10},{10,1... | collective-permute-start | bytes 786440 | tf_op jit(solution)/shard_map/ppermute | solution.py:14
  73.9 8.9 %collective-permute-start.7 = (f32[256,256]{0,1:T(8,128)S(1)}, f32[256,256]{0,1:T(8,128)S(1)}, u32[]{:S(2)}, u32[]{:S(2)}) collective-permute-start(f32[256,256]{0,1:T(8,128)S(1)} %fusion.163), channel_id=1, source_target_pairs={{0,1},{1,2},{2,3},{3,4},{4,5},{5,6},{6,7},{7,8},{8,9},{9,10},{10,1... | collective-permute-start | bytes 786440 | tf_op jit(solution)/shard_map/ppermute | solution.py:14
  83.7 8.9 %collective-permute-start.8 = (f32[256,256]{0,1:T(8,128)S(1)}, f32[256,256]{0,1:T(8,128)S(1)}, u32[]{:S(2)}, u32[]{:S(2)}) collective-permute-start(f32[256,256]{0,1:T(8,128)S(1)} %get-tuple-element.353), channel_id=1, source_target_pairs={{0,1},{1,2},{2,3},{3,4},{4,5},{5,6},{6,7},{7,8},{8,9},{9,10},{10,1... | collective-permute-start | bytes 786440 | tf_op jit(solution)/shard_map/ppermute | solution.py:14
  92.7 8.9 %collective-permute-start.9 = (f32[256,256]{0,1:T(8,128)S(1)}, f32[256,256]{0,1:T(8,128)S(1)}, u32[]{:S(2)}, u32[]{:S(2)}) collective-permute-start(f32[256,256]{0,1:T(8,128)S(1)} %select_select_fusion.2), channel_id=1, source_target_pairs={{0,1},{1,2},{2,3},{3,4},{4,5},{5,6},{6,7},{7,8},{8,9},{9,10},{10,1... | collective-permute-start | bytes 786440 | tf_op jit(solution)/shard_map/ppermute | solution.py:14
  101.6 8.9 %collective-permute-start.10 = (f32[256,256]{0,1:T(8,128)S(1)}, f32[256,256]{0,1:T(8,128)S(1)}, u32[]{:S(2)}, u32[]{:S(2)}) collective-permute-start(f32[256,256]{0,1:T(8,128)S(1)} %select_select_fusion.1), channel_id=1, source_target_pairs={{0,1},{1,2},{2,3},{3,4},{4,5},{5,6},{6,7},{7,8},{8,9},{9,10},{10,1... | collective-permute-start | bytes 786440 | tf_op jit(solution)/shard_map/ppermute | solution.py:14
  103.5 9.8 %collective-permute-start.12 = (f32[256,256]{0,1:T(8,128)S(1)}, f32[256,256]{0,1:T(8,128)S(1)}, u32[]{:S(2)}, u32[]{:S(2)}) collective-permute-start(f32[256,256]{0,1:T(8,128)S(1)} %get-tuple-element.354), channel_id=1, source_target_pairs={{0,1},{1,2},{2,3},{3,4},{4,5},{5,6},{6,7},{7,8},{8,9},{9,10},{10,1... | collective-permute-start | bytes 786440 | tf_op jit(solution)/shard_map/ppermute | solution.py:14
  110.6 8.9 %collective-permute-start.11 = (f32[256,256]{0,1:T(8,128)S(1)}, f32[256,256]{0,1:T(8,128)S(1)}, u32[]{:S(2)}, u32[]{:S(2)}) collective-permute-start(f32[256,256]{0,1:T(8,128)S(1)} %select_select_fusion), channel_id=1, source_target_pairs={{0,1},{1,2},{2,3},{3,4},{4,5},{5,6},{6,7},{7,8},{8,9},{9,10},{10,1... | collective-permute-start | bytes 786440 | tf_op jit(solution)/shard_map/ppermute | solution.py:14
  121.2 8.9 %collective-permute-start = (f32[256,256]{0,1:T(8,128)S(1)}, f32[256,256]{0,1:T(8,128)S(1)}, u32[]{:S(2)}, u32[]{:S(2)}) collective-permute-start(f32[256,256]{0,1:T(8,128)S(1)} %get-tuple-element.406), channel_id=1, source_target_pairs={{0,1},{1,2},{2,3},{3,4},{4,5},{5,6},{6,7},{7,8},{8,9},{9,10},{10,1... | collective-permute-start | bytes 786440 | tf_op jit(solution)/shard_map/while/body/eval_jaxpr/ppermute | solution.py:14
  130.1 8.9 %collective-permute-start = (f32[256,256]{0,1:T(8,128)S(1)}, f32[256,256]{0,1:T(8,128)S(1)}, u32[]{:S(2)}, u32[]{:S(2)}) collective-permute-start(f32[256,256]{0,1:T(8,128)S(1)} %get-tuple-element.406), channel_id=1, source_target_pairs={{0,1},{1,2},{2,3},{3,4},{4,5},{5,6},{6,7},{7,8},{8,9},{9,10},{10,1... | collective-permute-start | bytes 786440 | tf_op jit(solution)/shard_map/while/body/eval_jaxpr/ppermute | solution.py:14
  139.1 8.9 %collective-permute-start = (f32[256,256]{0,1:T(8,128)S(1)}, f32[256,256]{0,1:T(8,128)S(1)}, u32[]{:S(2)}, u32[]{:S(2)}) collective-permute-start(f32[256,256]{0,1:T(8,128)S(1)} %get-tuple-element.406), channel_id=1, source_target_pairs={{0,1},{1,2},{2,3},{3,4},{4,5},{5,6},{6,7},{7,8},{8,9},{9,10},{10,1... | collective-permute-start | bytes 786440 | tf_op jit(solution)/shard_map/while/body/eval_jaxpr/ppermute | solution.py:14
  148.1 8.9 %collective-permute-start = (f32[256,256]{0,1:T(8,128)S(1)}, f32[256,256]{0,1:T(8,128)S(1)}, u32[]{:S(2)}, u32[]{:S(2)}) collective-permute-start(f32[256,256]{0,1:T(8,128)S(1)} %get-tuple-element.406), channel_id=1, source_target_pairs={{0,1},{1,2},{2,3},{3,4},{4,5},{5,6},{6,7},{7,8},{8,9},{9,10},{10,1... | collective-permute-start | bytes 786440 | tf_op jit(solution)/shard_map/while/body/eval_jaxpr/ppermute | solution.py:14
  157.0 8.9 %collective-permute-start = (f32[256,256]{0,1:T(8,128)S(1)}, f32[256,256]{0,1:T(8,128)S(1)}, u32[]{:S(2)}, u32[]{:S(2)}) collective-permute-start(f32[256,256]{0,1:T(8,128)S(1)} %get-tuple-element.406), channel_id=1, source_target_pairs={{0,1},{1,2},{2,3},{3,4},{4,5},{5,6},{6,7},{7,8},{8,9},{9,10},{10,1... | collective-permute-start | bytes 786440 | tf_op jit(solution)/shard_map/while/body/eval_jaxpr/ppermute | solution.py:14
  166.0 8.9 %collective-permute-start = (f32[256,256]{0,1:T(8,128)S(1)}, f32[256,256]{0,1:T(8,128)S(1)}, u32[]{:S(2)}, u32[]{:S(2)}) collective-permute-start(f32[256,256]{0,1:T(8,128)S(1)} %get-tuple-element.406), channel_id=1, source_target_pairs={{0,1},{1,2},{2,3},{3,4},{4,5},{5,6},{6,7},{7,8},{8,9},{9,10},{10,1... | collective-permute-start | bytes 786440 | tf_op jit(solution)/shard_map/while/body/eval_jaxpr/ppermute | solution.py:14
  175.0 8.9 %collective-permute-start = (f32[256,256]{0,1:T(8,128)S(1)}, f32[256,256]{0,1:T(8,128)S(1)}, u32[]{:S(2)}, u32[]{:S(2)}) collective-permute-start(f32[256,256]{0,1:T(8,128)S(1)} %get-tuple-element.406), channel_id=1, source_target_pairs={{0,1},{1,2},{2,3},{3,4},{4,5},{5,6},{6,7},{7,8},{8,9},{9,10},{10,1... | collective-permute-start | bytes 786440 | tf_op jit(solution)/shard_map/while/body/eval_jaxpr/ppermute | solution.py:14
  183.9 8.9 %collective-permute-start = (f32[256,256]{0,1:T(8,128)S(1)}, f32[256,256]{0,1:T(8,128)S(1)}, u32[]{:S(2)}, u32[]{:S(2)}) collective-permute-start(f32[256,256]{0,1:T(8,128)S(1)} %get-tuple-element.406), channel_id=1, source_target_pairs={{0,1},{1,2},{2,3},{3,4},{4,5},{5,6},{6,7},{7,8},{8,9},{9,10},{10,1... | collective-permute-start | bytes 786440 | tf_op jit(solution)/shard_map/while/body/eval_jaxpr/ppermute | solution.py:14
  192.9 8.9 %collective-permute-start = (f32[256,256]{0,1:T(8,128)S(1)}, f32[256,256]{0,1:T(8,128)S(1)}, u32[]{:S(2)}, u32[]{:S(2)}) collective-permute-start(f32[256,256]{0,1:T(8,128)S(1)} %get-tuple-element.406), channel_id=1, source_target_pairs={{0,1},{1,2},{2,3},{3,4},{4,5},{5,6},{6,7},{7,8},{8,9},{9,10},{10,1... | collective-permute-start | bytes 786440 | tf_op jit(solution)/shard_map/while/body/eval_jaxpr/ppermute | solution.py:14
  201.9 8.9 %collective-permute-start = (f32[256,256]{0,1:T(8,128)S(1)}, f32[256,256]{0,1:T(8,128)S(1)}, u32[]{:S(2)}, u32[]{:S(2)}) collective-permute-start(f32[256,256]{0,1:T(8,128)S(1)} %get-tuple-element.406), channel_id=1, source_target_pairs={{0,1},{1,2},{2,3},{3,4},{4,5},{5,6},{6,7},{7,8},{8,9},{9,10},{10,1... | collective-permute-start | bytes 786440 | tf_op jit(solution)/shard_map/while/body/eval_jaxpr/ppermute | solution.py:14
  210.9 8.9 %collective-permute-start = (f32[256,256]{0,1:T(8,128)S(1)}, f32[256,256]{0,1:T(8,128)S(1)}, u32[]{:S(2)}, u32[]{:S(2)}) collective-permute-start(f32[256,256]{0,1:T(8,128)S(1)} %get-tuple-element.406), channel_id=1, source_target_pairs={{0,1},{1,2},{2,3},{3,4},{4,5},{5,6},{6,7},{7,8},{8,9},{9,10},{10,1... | collective-permute-start | bytes 786440 | tf_op jit(solution)/shard_map/while/body/eval_jaxpr/ppermute | solution.py:14
  219.8 8.9 %collective-permute-start = (f32[256,256]{0,1:T(8,128)S(1)}, f32[256,256]{0,1:T(8,128)S(1)}, u32[]{:S(2)}, u32[]{:S(2)}) collective-permute-start(f32[256,256]{0,1:T(8,128)S(1)} %get-tuple-element.406), channel_id=1, source_target_pairs={{0,1},{1,2},{2,3},{3,4},{4,5},{5,6},{6,7},{7,8},{8,9},{9,10},{10,1... | collective-permute-start | bytes 786440 | tf_op jit(solution)/shard_map/while/body/eval_jaxpr/ppermute | solution.py:14
  228.8 8.9 %collective-permute-start = (f32[256,256]{0,1:T(8,128)S(1)}, f32[256,256]{0,1:T(8,128)S(1)}, u32[]{:S(2)}, u32[]{:S(2)}) collective-permute-start(f32[256,256]{0,1:T(8,128)S(1)} %get-tuple-element.406), channel_id=1, source_target_pairs={{0,1},{1,2},{2,3},{3,4},{4,5},{5,6},{6,7},{7,8},{8,9},{9,10},{10,1... | collective-permute-start | bytes 786440 | tf_op jit(solution)/shard_map/while/body/eval_jaxpr/ppermute | solution.py:14
  237.8 8.9 %collective-permute-start = (f32[256,256]{0,1:T(8,128)S(1)}, f32[256,256]{0,1:T(8,128)S(1)}, u32[]{:S(2)}, u32[]{:S(2)}) collective-permute-start(f32[256,256]{0,1:T(8,128)S(1)} %get-tuple-element.406), channel_id=1, source_target_pairs={{0,1},{1,2},{2,3},{3,4},{4,5},{5,6},{6,7},{7,8},{8,9},{9,10},{10,1... | collective-permute-start | bytes 786440 | tf_op jit(solution)/shard_map/while/body/eval_jaxpr/ppermute | solution.py:14
  246.7 8.9 %collective-permute-start = (f32[256,256]{0,1:T(8,128)S(1)}, f32[256,256]{0,1:T(8,128)S(1)}, u32[]{:S(2)}, u32[]{:S(2)}) collective-permute-start(f32[256,256]{0,1:T(8,128)S(1)} %get-tuple-element.406), channel_id=1, source_target_pairs={{0,1},{1,2},{2,3},{3,4},{4,5},{5,6},{6,7},{7,8},{8,9},{9,10},{10,1... | collective-permute-start | bytes 786440 | tf_op jit(solution)/shard_map/while/body/eval_jaxpr/ppermute | solution.py:14
  255.7 8.9 %collective-permute-start.13 = (f32[256,256]{0,1:T(8,128)S(1)}, f32[256,256]{0,1:T(8,128)S(1)}, u32[]{:S(2)}, u32[]{:S(2)}) collective-permute-start(f32[256,256]{0,1:T(8,128)S(1)} %subtract_select_fusion), channel_id=1, source_target_pairs={{0,1},{1,2},{2,3},{3,4},{4,5},{5,6},{6,7},{7,8},{8,9},{9,10},{10,1... | collective-permute-start | bytes 786440 | tf_op jit(solution)/shard_map/ppermute | solution.py:14
  266.9 8.9 %collective-permute-start.14 = (f32[256,256]{0,1:T(8,128)S(1)}, f32[256,256]{0,1:T(8,128)S(1)}, u32[]{:S(2)}, u32[]{:S(2)}) collective-permute-start(f32[256,256]{0,1:T(8,128)S(1)} %fusion.167), channel_id=1, source_target_pairs={{0,1},{1,2},{2,3},{3,4},{4,5},{5,6},{6,7},{7,8},{8,9},{9,10},{10,1... | collective-permute-start | bytes 786440 | tf_op jit(solution)/shard_map/ppermute | solution.py:14
  276.7 8.9 %collective-permute-start.15 = (f32[256,256]{0,1:T(8,128)S(1)}, f32[256,256]{0,1:T(8,128)S(1)}, u32[]{:S(2)}, u32[]{:S(2)}) collective-permute-start(f32[256,256]{0,1:T(8,128)S(1)} %fusion.168), channel_id=1, source_target_pairs={{0,1},{1,2},{2,3},{3,4},{4,5},{5,6},{6,7},{7,8},{8,9},{9,10},{10,1... | collective-permute-start | bytes 786440 | tf_op jit(solution)/shard_map/ppermute | solution.py:14
  286.5 8.9 %collective-permute-start.16 = (f32[256,256]{0,1:T(8,128)S(1)}, f32[256,256]{0,1:T(8,128)S(1)}, u32[]{:S(2)}, u32[]{:S(2)}) collective-permute-start(f32[256,256]{0,1:T(8,128)S(1)} %fusion.174), channel_id=1, source_target_pairs={{0,1},{1,2},{2,3},{3,4},{4,5},{5,6},{6,7},{7,8},{8,9},{9,10},{10,1... | collective-permute-start | bytes 786440 | tf_op jit(solution)/shard_map/ppermute | solution.py:14
  (6 other events, 50.3 us)
where the time goes:
time: 300 us; the launch traced here: 299 us
  waiting for transfers between devices  207 us (69%)
  starting transfers between devices  59.7 us (20%)
  matrix products  19.8 us (7%)
  local copies, waits for them, and re-layouts  8.61 us (3%)
    ppermute x31, waiting for transfers between devices, passed_along(): return lax.ppermute(x, axis, pairs)  207 us
    ppermute x31, starting transfers between devices, passed_along(): return lax.ppermute(x, axis, pairs)  59.7 us
    dot_general x22, matrix products, convolve(): return jnp.dot(weight, stacked, preferred_element_type=jnp.float32)  19.8 us
  transfers between devices with their start and end apart: 31, of which 31 were waited for; matrix products, arithmetic and copies ran while one was open for 0% of the time, Pallas kernels for 0%

commit v1 on v0

v1 whole, which is shorter than its diff:
```python
import functools

import jax
import jax.numpy as jnp
from jax import lax
from jax.experimental import pallas as pl
from jax.experimental.pallas import tpu as pltpu
from jax.sharding import PartitionSpec as P

SIDE = 16
CELLS = 256
CHANS = 256
TAPS = 9 * CHANS
COARSEN = 4
DEVICES = 16
F32 = jnp.float32
BF16 = jnp.bfloat16
STATE = (CELLS, CHANS)
VMEM_LIMIT = 28 << 20


def conv_tanh(state, weight):
    column = lax.broadcasted_iota(jnp.int32, STATE, 0) % SIDE
    before = jnp.where(column == 0, 0.0, pltpu.roll(state, 1, 0)).astype(BF16)
    after = jnp.where(column == SIDE - 1, 0.0, pltpu.roll(state, CELLS - 1, 0)).astype(BF16)
    trio = [before, state.astype(BF16), after]
    edge = jnp.zeros((SIDE, CHANS), BF16)
    above = [jnp.concatenate([edge, x[:-SIDE]], 0) for x in trio]
    below = [jnp.concatenate([x[SIDE:], edge], 0) for x in trio]
    total = None
    for tap, piece in enumerate(above + trio + below):
        part = lax.dot_general(
            piece,
            weight[:, tap * CHANS : (tap + 1) * CHANS],
            (((1,), (1,)), ((), ())),
            preferred_element_type=F32,
        )
        total = part if total is None else total + part
    return jnp.tanh(total)


def vmem(shape, dtype):
    return pltpu.VMEM(shape, dtype)


def kernel_call(body, outs, args, name, steps, anywhere=(), scratch=()):
    args = [
        a if i in anywhere else pltpu.with_memory_space_constraint(a, pltpu.VMEM)
        for i, a in enumerate(args)
    ]
    return pl.pallas_call(
        body,
        out_shape=outs,
        in_specs=[
            pl.BlockSpec(memory_space=pl.ANY if i in anywhere else pltpu.VMEM)
            for i in range(len(args))
        ],
        out_specs=[pl.BlockSpec(memory_space=pltpu.VMEM) for _ in outs],
        scratch_shapes=list(scratch),
        compiler_params=pltpu.CompilerParams(vmem_limit_bytes=VMEM_LIMIT),
        cost_estimate=pl.CostEstimate(
            flops=steps * 2 * TAPS * CELLS * CHANS, bytes_accessed=1 << 20, transcendentals=0
        ),
        name=name,
    )(*args)


def place():
    return lax.axis_index("layer")


def first_sweep(inputs, guess, weights, cpoint, held, start, sems):
    copies = [
        pltpu.make_async_copy(weights.at[i], held.at[i], sems.at[i]) for i in range(COARSEN)
    ]
    for copy in copies:
        copy.start()
    start[...] = inputs[...].T
    state = jnp.where(place() == 0, inputs[...], guess[0]).T
    for i in range(COARSEN):
        copies[i].wait()
        state = state + 0.25 * conv_tanh(state, held[i])
    cpoint[...] = state.astype(BF16)


def second_sweep(left, start, held, rhs, pack):
    state = jnp.where(place() == 0, start[...], left[...].astype(F32))
    terms = []
    for i in range(COARSEN):
        terms.append(conv_tanh(state, held[i]))
        state = state + 0.25 * terms[-1]
    own = 0.25 * (terms[0] + terms[1] + terms[2] + terms[3]) - terms[0]
    rhs[...] = own
    pack[0] = state
    pack[1] = own


def stage1(pack, rhs, held, out):
    @pl.when(place() % 4 == 1)
    def _():
        first = pack[0]
        out[...] = (first + conv_tanh(first, held[0]) + rhs[...]).astype(BF16)


def both_steps(value, pack, rhs, even_w, held):
    value = value + conv_tanh(value, even_w[...]) + pack[1]
    return value + conv_tanh(value, held[0]) + rhs[...]


def stage2(got, pack, rhs, even_w, held, out, wide):
    @pl.when(place() % 4 == 3)
    def _():
        value = both_steps(got[...].astype(F32), pack, rhs, even_w, held)
        wide[...] = value
        out[...] = value.astype(BF16)


def stage3(got, upper, pack, rhs, even_w, held, out, xi):
    me = place()

    @pl.when((me % 4 == 1) & (me > 4))
    def _():
        out[...] = both_steps(got[...].astype(F32), pack, rhs, even_w, held).astype(BF16)

    @pl.when((me % 4 == 3) & (me > 4))
    def _():
        value = upper[...].astype(F32)
        xi[...] = value + 4.0 * conv_tanh(value, held[0])


def stage4(got, xi, pack, rhs, even_w, held, out, wide, second):
    me = place()

    @pl.when((me % 4 == 3) & (me > 4))
    def _():
        value = both_steps(got[...].astype(F32), pack, rhs, even_w, held)
        wide[...] = value
        out[...] = value.astype(BF16)
        second[...] = value - xi[...]


def stage56(owner, runner, got, carried, second, pack, rhs, even_w, held, out, wide):
    me = place()

    @pl.when(me == owner)
    def _():
        value = got[...].astype(F32)
        value = value + 4.0 * conv_tanh(value, held[0]) + second[...]
        wide[...] = value
        out[...] = value.astype(BF16)

    @pl.when(me == runner)
    def _():
        out[...] = both_steps(carried[...].astype(F32), pack, rhs, even_w, held).astype(BF16)


def last_sweep(last, final, start, solved1, solved2, solved3, solved4, pack, rhs, even_w, held, states, left):
    me = place()

    @pl.when(me == 0)
    def _():
        left[...] = start[...]

    @pl.when((me % 2 == 0) & (me > 0))
    def _():
        left[...] = jnp.where(me == 14, last[...], final[...]).astype(F32)

    @pl.when(me % 2 == 1)
    def _():
        value = jnp.where(me == 15, last[...], final[...]).astype(F32)
        value = jnp.where(me == 1, start[...], value)
        left[...] = value + conv_tanh(value, even_w[...]) + pack[1]

    state = left[...]
    term = conv_tanh(state, held[0])
    left[...] = state + term + rhs[...]
    for owner, solved in ((3, solved1), (7, solved2), (11, solved3), (15, solved4)):

        @pl.when(me == owner)
        def _():
            left[...] = solved[...]

    states[3] = left[...].T
    state = state + 0.25 * term
    states[0] = state.T
    for i in range(1, COARSEN - 1):
        state = state + 0.25 * conv_tanh(state, held[i])
        states[i] = state.T


def per_device(inputs, guess, weights):
    me = lax.axis_index("layer")

    def send(value, pairs):
        return lax.ppermute(value, "layer", pairs)

    narrow = vmem(STATE, BF16)
    wide = vmem(STATE, F32)
    intra_up = [(i, i + 1) for i in range(0, DEVICES, 2)]

    even_w = send(weights[0], intra_up)
    cpoint, held, start = kernel_call(
        first_sweep,
        [narrow, vmem((COARSEN, CHANS, TAPS), BF16), wide],
        [inputs, guess, weights],
        "first_sweep",
        4,
        anywhere=(2,),
        scratch=[pltpu.SemaphoreType.DMA((COARSEN,))],
    )
    left = send(cpoint, [(i, i + 1) for i in range(DEVICES - 1)])
    rhs, pack = kernel_call(
        second_sweep, [wide, vmem((2, *STATE), F32)], [left, start, held], "second_sweep", 4
    )
    pack = send(pack, intra_up)
    common = [pack, rhs, even_w, held]

    (c1,) = kernel_call(stage1, [narrow], [pack, rhs, held], "stage1", 1)
    got3 = send(c1, [(1, 3), (5, 7), (9, 11), (13, 15)])
    upper, wide1 = kernel_call(stage2, [narrow, wide], [got3, *common], "stage2", 2)
    got4 = send(upper, [(3, 5), (7, 9), (11, 13)])
    upper_prev = send(upper, [(3, 7), (7, 11), (11, 15)])
    c2, xi = kernel_call(stage3, [narrow, wide], [got4, upper_prev, *common], "stage3", 2)
    got5 = send(c2, [(5, 7), (9, 11), (13, 15)])
    z2, wide2, second = kernel_call(
        stage4, [narrow, wide, wide], [got5, xi, *common], "stage4", 2
    )
    got6 = send(z2, [(7, 11)])
    got6b = send(z2, [(7, 9)])
    z3, wide3 = kernel_call(
        functools.partial(stage56, 11, 9),
        [narrow, wide],
        [got6, got6b, second, *common],
        "stage5",
        2,
    )
    got7 = send(z3, [(11, 13), (9, 11)])
    got7b = send(z3, [(11, 15)])
    z4, wide4 = kernel_call(
        functools.partial(stage56, 15, 13),
        [narrow, wide],
        [got7b, got7, second, *common],
        "stage6",
        2,
    )
    got8 = send(z4, [(13, 15)])
    got8b = send(z4, [(13, 14)])
    final = got3
    for chip, got in ((2, got4), (3, got5), (4, got6b), (5, got7), (6, got7)):
        final = jnp.where(me == 2 * chip + 1, got, final)
    handed = send(final, [(2 * chip + 1, 2 * chip) for chip in range(1, 7)])
    final = jnp.where(me % 2 == 0, handed, final)
    last = jnp.where(me == 14, got8b, got8)
    return kernel_call(
        last_sweep,
        [jax.ShapeDtypeStruct((COARSEN, CHANS, CELLS), F32)],
        [last, final, start, wide1, wide2, wide3, wide4, *common],
        "last_sweep",
        4,
        scratch=[pltpu.VMEM(STATE, F32)],
    )[0]


def solution(mesh):
    return jax.shard_map(
        per_device,
        mesh=mesh,
        in_specs=(P(None, "batch"), P("layer", None, "batch"), P("layer", None, None)),
        out_specs=P("layer", None, "batch"),
        check_vma=False,
    )
```

time: 300 us -> 80.1 us (0.27)
  the two profiles are of different devices: /device:TPU:138 before, /device:TPU:248 now
where the time goes in v1:
time: 80.1 us; the launch traced here: 79.5 us
  waiting for transfers between devices  43.5 us (54%)
  starting transfers between devices  13.8 us (17%)
  Pallas kernels  11 us (14%)
  local copies, waits for them, and re-layouts  9.33 us (12%)
  other arithmetic  1.63 us (2%)
    ppermute x14, waiting for transfers between devices, send(): return lax.ppermute(value, 'layer', pairs)  43.5 us
    ppermute x14, starting transfers between devices, send(): return lax.ppermute(value, 'layer', pairs)  13.8 us
    pallas_call x9, Pallas kernels, kernel_call(): pl.pallas_call(body, out_shape=outs, in_specs=[pl.BlockSpec(memory_space=...  11 us
    unnamed x18, local copies, waits for them, and re-layouts  7.98 us
  transfers between devices with their start and end apart: 14, of which 3 were waited for; matrix products, arithmetic and copies ran while one was open for 2% of the time, Pallas kernels for 9%

profile of v1, /device:TPU:248, one launch (start us, length us, event | category | flops | bytes accessed | tf_op | source)
XLA Modules:
  0.0 79.5 jit_solution(3762091299324299082)
XLA Ops:
  0.0 1.3 %slice_bitcast_fusion = bf16[256,2304]{1,0:T(8,128)(2,1)S(1)} fusion(bf16[4,256,2304]{2,1,0:T(8,128)(2,1)} %weights.1), kind=kLoop, calls=%fused_computation | loop fusion | bytes 2359296 | tf_op jit(solution)/shard_map/squeeze | solution.py:201
  1.4 1.8 %collective-permute-start.3 = (bf16[256,2304]{1,0:T(8,128)(2,1)S(1)}, bf16[256,2304]{1,0:T(8,128)(2,1)S(1)}, u32[]{:S(2)}, u32[]{:S(2)}) collective-permute-start(bf16[256,2304]{1,0:T(8,128)(2,1)S(1)} %slice_bitcast_fusion), channel_id=1, source_target_pairs={{0,1},{2,3},{4,5},{6,7},{8,9},{10,11},{12,13},{14,15},{16,17},{18,... | collective-permute-start | bytes 3538952 | tf_op jit(solution)/shard_map/ppermute | solution.py:195
  3.2 0.0 copy-start.2
  3.2 2.3 %copy-done.2 = bf16[4,256,2304]{2,1,0:T(8,128)(2,1)S(1)} copy-done((bf16[4,256,2304]{2,1,0:T(8,128)(2,1)S(1)}, bf16[4,256,2304]{2,1,0:T(8,128)(2,1)}, u32[]{:S(2)}) %copy-start.2) | copy-done | bytes 4718616
  5.5 0.9 %copy-done.3 = f32[256,256]{1,0:T(8,128)S(1)} copy-done((f32[256,256]{1,0:T(8,128)S(1)}, f32[256,256]{1,0:T(8,128)}, u32[]{:S(2)}) %copy-start.3) | copy-done | bytes 262168
  6.5 0.9 %copy-done.4 = f32[1,256,256]{2,1,0:T(8,128)S(1)} copy-done((f32[1,256,256]{2,1,0:T(8,128)S(1)}, f32[1,256,256]{2,1,0:T(8,128)}, u32[]{:S(2)}) %copy-start.4) | copy-done | bytes 262168
  7.4 4.4 %first_sweep.1 = (bf16[256,256]{1,0:T(8,128)(2,1)S(1)}, bf16[4,256,2304]{2,1,0:T(8,128)(2,1)S(1)}, f32[256,256]{1,0:T(8,128)S(1)}) custom-call(f32[256,256]{1,0:T(8,128)S(1)} %copy-done.3, f32[1,256,256]{2,1,0:T(8,128)S(1)} %copy-done.4, bf16[4,256,2304]{2,1,0:T(8,128)(2,1)S(1)} %copy-done.2), custom_call_target="tpu_custom_call" | custom-call | flops 1207959552 | bytes 1048576 | tf_op jit(solution)/shard_map/first_sweep/pallas_call | solution.py:51
  11.8 1.9 %collective-permute-start = (bf16[256,256]{1,0:T(8,128)(2,1)S(1)}, bf16[256,256]{1,0:T(8,128)(2,1)S(1)}, u32[]{:S(2)}, u32[]{:S(2)}) collective-permute-start(bf16[256,256]{1,0:T(8,128)(2,1)S(1)} %get-tuple-element.21), channel_id=1, source_target_pairs={{0,1},{1,2},{2,3},{3,4},{4,5},{5,6},{6,7},{7,8},{8,9},{9,10},{10,1... | collective-permute-start | bytes 393224 | tf_op jit(solution)/shard_map/ppermute | solution.py:195
  13.7 4.4 %collective-permute-done.left = bf16[256,256]{1,0:T(8,128)(2,1)S(1)} collective-permute-done((bf16[256,256]{1,0:T(8,128)(2,1)S(1)}, bf16[256,256]{1,0:T(8,128)(2,1)S(1)}, u32[]{:S(2)}, u32[]{:S(2)}) %collective-permute-start) | collective-permute-done | bytes 131104 | tf_op jit(solution)/shard_map/ppermute | solution.py:195
  18.1 2.8 %second_sweep.1 = (f32[256,256]{1,0:T(8,128)S(1)}, f32[2,256,256]{2,1,0:T(8,128)S(1)}) custom-call(bf16[256,256]{1,0:T(8,128)(2,1)S(1)} %collective-permute-done.left, f32[256,256]{1,0:T(8,128)S(1)} %get-tuple-element.22.start, bf16[4,256,2304]{2,1,0:T(8,128)(2,1)S(1)} %get-tuple-element.23.held), custom_call_target="tpu_custom_call" | custom-call | flops 1207959552 | bytes 1048576 | tf_op jit(solution)/shard_map/second_sweep/pallas_call | solution.py:51
  20.9 1.3 %collective-permute-start.1 = (f32[2,256,256]{2,1,0:T(8,128)S(1)}, f32[2,256,256]{2,1,0:T(8,128)S(1)}, u32[]{:S(2)}, u32[]{:S(2)}) collective-permute-start(f32[2,256,256]{2,1,0:T(8,128)S(1)} %get-tuple-element.24), channel_id=1, source_target_pairs={{0,1},{2,3},{4,5},{6,7},{8,9},{10,11},{12,13},{14,15},{16,17},{18,... | collective-permute-start | bytes 1572872 | tf_op jit(solution)/shard_map/ppermute | solution.py:195
  22.2 1.5 %collective-permute-done.1.pack = f32[2,256,256]{2,1,0:T(8,128)S(1)} collective-permute-done((f32[2,256,256]{2,1,0:T(8,128)S(1)}, f32[2,256,256]{2,1,0:T(8,128)S(1)}, u32[]{:S(2)}, u32[]{:S(2)}) %collective-permute-start.1) | collective-permute-done | bytes 524320 | tf_op jit(solution)/shard_map/ppermute | solution.py:195
  23.7 0.7 collective-permute-start.2
  24.4 0.7 collective-permute-start.5
  25.1 0.7 collective-permute-start.4
  25.8 0.7 collective-permute-start.6
  26.5 0.0 copy-start.5
  26.6 0.7 copy-done.5
  27.2 0.7 collective-permute-start.8
  27.9 0.7 collective-permute-start.7
  28.6 0.7 stage5.1
  29.3 0.7 copy-done.7
  30.0 0.7 collective-permute-start.10
  30.7 0.7 collective-permute-start.9
  31.4 0.7 select_select_fusion
  32.1 1.3 %collective-permute-start.13 = (bf16[256,256]{1,0:T(8,128)(2,1)}, bf16[256,256]{1,0:T(8,128)(2,1)}, u32[]{:S(2)}, u32[]{:S(2)}) collective-permute-start(bf16[256,256]{1,0:T(8,128)(2,1)} %select_select_fusion), channel_id=1, source_target_pairs={{3,2},{5,4},{7,6},{9,8},{11,10},{13,12},{19,18},{21,20},{23,22},{2... | collective-permute-start | bytes 393224 | tf_op jit(solution)/shard_map/ppermute | solution.py:195
  33.4 2.3 %copy-done.1 = bf16[4,256,2304]{2,1,0:T(8,128)(2,1)S(1)} copy-done((bf16[4,256,2304]{2,1,0:T(8,128)(2,1)S(1)}, bf16[4,256,2304]{2,1,0:T(8,128)(2,1)}, u32[]{:S(2)}) %copy-start.1) | copy-done | bytes 4718616
  35.7 0.8 collective-permute-start.12
  36.5 1.3 %collective-permute-start.11 = (bf16[256,256]{1,0:T(8,128)(2,1)S(1)}, bf16[256,256]{1,0:T(8,128)(2,1)S(1)}, u32[]{:S(2)}, u32[]{:S(2)}) collective-permute-start(bf16[256,256]{1,0:T(8,128)(2,1)S(1)} %get-tuple-element.32), channel_id=1, source_target_pairs={{13,14},{29,30},{45,46},{61,62},{77,78},{93,94},{109,110},{125,126... | collective-permute-start | bytes 393224 | tf_op jit(solution)/shard_map/ppermute | solution.py:195
  37.8 0.9 %broadcast_select_fusion.final = bf16[256,256]{1,0:T(8,128)(2,1)S(1)} fusion(bf16[256,256]{1,0:T(8,128)(2,1)} %collective-permute-done.13, bf16[256,256]{1,0:T(8,128)(2,1)} %select_select_fusion, pred[]{:T(512)S(6)} %eq.24), kind=kLoop, calls=%fused_computation.2 | loop fusion | flops 65536 | bytes 393217 | tf_op jit(solution)/shard_map/jit(_where)/select_n | solution.py:252
  38.8 37.6 %collective-permute-done.11 = bf16[256,256]{1,0:T(8,128)(2,1)S(1)} collective-permute-done((bf16[256,256]{1,0:T(8,128)(2,1)S(1)}, bf16[256,256]{1,0:T(8,128)(2,1)S(1)}, u32[]{:S(2)}, u32[]{:S(2)}) %collective-permute-start.11) | collective-permute-done | bytes 131104 | tf_op jit(solution)/shard_map/ppermute | solution.py:195
  76.4 3.1 %last_sweep.1 = f32[4,256,256]{2,1,0:T(8,128)} custom-call(bf16[256,256]{1,0:T(8,128)(2,1)S(1)} %broadcast_select_fusion.1.last, bf16[256,256]{1,0:T(8,128)(2,1)S(1)} %broadcast_select_fusion.final, f32[256,256]{1,0:T(8,128)S(1)} %get-tuple-element.22.start, f32[256,256]{1,0:T(8,128)S(1)} %get-tuple-element.33.solved1, f32[256,256]{1,0:T(8,128)S(1)} %copy-done.6, ...), custom_call_target="tpu_custom_call" | custom-call | flops 1207959552 | bytes 1048576 | tf_op jit(solution)/shard_map/last_sweep/pallas_call | solution.py:51
  (27 shorter events, 0.1 us)
Async XLA Ops:
  1.4 23.0 %collective-permute-start.3 = (bf16[256,2304]{1,0:T(8,128)(2,1)S(1)}, bf16[256,2304]{1,0:T(8,128)(2,1)S(1)}, u32[]{:S(2)}, u32[]{:S(2)}) collective-permute-start(bf16[256,2304]{1,0:T(8,128)(2,1)S(1)} %slice_bitcast_fusion), channel_id=1, source_target_pairs={{0,1},{2,3},{4,5},{6,7},{8,9},{10,11},{12,13},{14,15},{16,17},{18,... | collective-permute-start | bytes 3538952 | tf_op jit(solution)/shard_map/ppermute | solution.py:195
  3.2 2.3 %copy-start.2 = (bf16[4,256,2304]{2,1,0:T(8,128)(2,1)S(1)}, bf16[4,256,2304]{2,1,0:T(8,128)(2,1)}, u32[]{:S(2)}) copy-start(bf16[4,256,2304]{2,1,0:T(8,128)(2,1)} %weights.1) | copy-start | bytes 14155780
  5.5 0.9 %copy-start.3 = (f32[256,256]{1,0:T(8,128)S(1)}, f32[256,256]{1,0:T(8,128)}, u32[]{:S(2)}) copy-start(f32[256,256]{1,0:T(8,128)} %inputs.1) | copy-start | bytes 786436
  6.5 0.9 %copy-start.4 = (f32[1,256,256]{2,1,0:T(8,128)S(1)}, f32[1,256,256]{2,1,0:T(8,128)}, u32[]{:S(2)}) copy-start(f32[1,256,256]{2,1,0:T(8,128)} %guess.1) | copy-start | bytes 786436
  11.8 16.8 %copy-start = (bf16[4,256,2304]{2,1,0:T(8,128)(2,1)}, bf16[4,256,2304]{2,1,0:T(8,128)(2,1)S(1)}, u32[]{:S(2)}) copy-start(bf16[4,256,2304]{2,1,0:T(8,128)(2,1)S(1)} %get-tuple-element.23.held) | copy-start | bytes 14155780
  11.8 6.3 %collective-permute-start = (bf16[256,256]{1,0:T(8,128)(2,1)S(1)}, bf16[256,256]{1,0:T(8,128)(2,1)S(1)}, u32[]{:S(2)}, u32[]{:S(2)}) collective-permute-start(bf16[256,256]{1,0:T(8,128)(2,1)S(1)} %get-tuple-element.21), channel_id=1, source_target_pairs={{0,1},{1,2},{2,3},{3,4},{4,5},{5,6},{6,7},{7,8},{8,9},{9,10},{10,1... | collective-permute-start | bytes 393224 | tf_op jit(solution)/shard_map/ppermute | solution.py:195
  20.9 2.8 %collective-permute-start.1 = (f32[2,256,256]{2,1,0:T(8,128)S(1)}, f32[2,256,256]{2,1,0:T(8,128)S(1)}, u32[]{:S(2)}, u32[]{:S(2)}) collective-permute-start(f32[2,256,256]{2,1,0:T(8,128)S(1)} %get-tuple-element.24), channel_id=1, source_target_pairs={{0,1},{2,3},{4,5},{6,7},{8,9},{10,11},{12,13},{14,15},{16,17},{18,... | collective-permute-start | bytes 1572872 | tf_op jit(solution)/shard_map/ppermute | solution.py:195
  23.7 0.7 collective-permute-start.2
  24.4 1.4 %collective-permute-start.5 = (bf16[256,256]{1,0:T(8,128)(2,1)S(1)}, bf16[256,256]{1,0:T(8,128)(2,1)S(1)}, u32[]{:S(2)}, u32[]{:S(2)}) collective-permute-start(bf16[256,256]{1,0:T(8,128)(2,1)S(1)} %get-tuple-element.26), channel_id=1, source_target_pairs={{3,7},{7,11},{11,15},{19,23},{23,27},{27,31},{35,39},{39,43},{43,4... | collective-permute-start | bytes 393224 | tf_op jit(solution)/shard_map/ppermute | solution.py:195
  25.1 0.7 collective-permute-start.4
  25.8 0.7 collective-permute-start.6
  26.5 0.7 copy-start.5
  27.2 1.3 %collective-permute-start.8 = (bf16[256,256]{1,0:T(8,128)(2,1)S(1)}, bf16[256,256]{1,0:T(8,128)(2,1)S(1)}, u32[]{:S(2)}, u32[]{:S(2)}) collective-permute-start(bf16[256,256]{1,0:T(8,128)(2,1)S(1)} %get-tuple-element.29), channel_id=1, source_target_pairs={{7,9},{23,25},{39,41},{55,57},{71,73},{87,89},{103,105},{119,121},... | collective-permute-start | bytes 393224 | tf_op jit(solution)/shard_map/ppermute | solution.py:195
  27.9 0.7 collective-permute-start.7
  29.3 0.7 copy-start.7
  30.0 1.4 %collective-permute-start.10 = (bf16[256,256]{1,0:T(8,128)(2,1)}, bf16[256,256]{1,0:T(8,128)(2,1)S(1)}, u32[]{:S(2)}, u32[]{:S(2)}) collective-permute-start(bf16[256,256]{1,0:T(8,128)(2,1)} %get-tuple-element.31), channel_id=1, source_target_pairs={{11,13},{9,11},{27,29},{25,27},{43,45},{41,43},{59,61},{57,59},{75... | collective-permute-start | bytes 393224 | tf_op jit(solution)/shard_map/ppermute | solution.py:195
  30.7 2.7 %collective-permute-start.9 = (bf16[256,256]{1,0:T(8,128)(2,1)}, bf16[256,256]{1,0:T(8,128)(2,1)S(1)}, u32[]{:S(2)}, u32[]{:S(2)}) collective-permute-start(bf16[256,256]{1,0:T(8,128)(2,1)} %get-tuple-element.31), channel_id=1, source_target_pairs={{11,15},{27,31},{43,47},{59,63},{75,79},{91,95},{107,111},{123,127... | collective-permute-start | bytes 393224 | tf_op jit(solution)/shard_map/ppermute | solution.py:195
  32.1 5.8 %collective-permute-start.13 = (bf16[256,256]{1,0:T(8,128)(2,1)}, bf16[256,256]{1,0:T(8,128)(2,1)}, u32[]{:S(2)}, u32[]{:S(2)}) collective-permute-start(bf16[256,256]{1,0:T(8,128)(2,1)} %select_select_fusion), channel_id=1, source_target_pairs={{3,2},{5,4},{7,6},{9,8},{11,10},{13,12},{19,18},{21,20},{23,22},{2... | collective-permute-start | bytes 393224 | tf_op jit(solution)/shard_map/ppermute | solution.py:195
  33.4 2.3 %copy-start.1 = (bf16[4,256,2304]{2,1,0:T(8,128)(2,1)S(1)}, bf16[4,256,2304]{2,1,0:T(8,128)(2,1)}, u32[]{:S(2)}) copy-start(bf16[4,256,2304]{2,1,0:T(8,128)(2,1)} %copy-done) | copy-start | bytes 14155780
  35.7 40.7 %copy-start.6 = (f32[256,256]{1,0:T(8,128)S(1)}, f32[256,256]{1,0:T(8,128)}, u32[]{:S(2)}) copy-start(f32[256,256]{1,0:T(8,128)} %copy-done.5) | copy-start | bytes 786436
  35.7 40.7 %copy-start.8 = (f32[256,256]{1,0:T(8,128)S(1)}, f32[256,256]{1,0:T(8,128)}, u32[]{:S(2)}) copy-start(f32[256,256]{1,0:T(8,128)} %copy-done.7) | copy-start | bytes 786436
  35.7 3.0 %collective-permute-start.12 = (bf16[256,256]{1,0:T(8,128)(2,1)S(1)}, bf16[256,256]{1,0:T(8,128)(2,1)S(1)}, u32[]{:S(2)}, u32[]{:S(2)}) collective-permute-start(bf16[256,256]{1,0:T(8,128)(2,1)S(1)} %get-tuple-element.32), channel_id=1, source_target_pairs={{13,15},{29,31},{45,47},{61,63},{77,79},{93,95},{109,111},{125,127... | collective-permute-start | bytes 393224 | tf_op jit(solution)/shard_map/ppermute | solution.py:195
  36.5 39.9 %collective-permute-start.11 = (bf16[256,256]{1,0:T(8,128)(2,1)S(1)}, bf16[256,256]{1,0:T(8,128)(2,1)S(1)}, u32[]{:S(2)}, u32[]{:S(2)}) collective-permute-start(bf16[256,256]{1,0:T(8,128)(2,1)S(1)} %get-tuple-element.32), channel_id=1, source_target_pairs={{13,14},{29,30},{45,46},{61,62},{77,78},{93,94},{109,110},{125,126... | collective-permute-start | bytes 393224 | tf_op jit(solution)/shard_map/ppermute | solution.py:195
